TPU v7x, 32 devices: a whole 2x2x4 slice. The times are simulated.
32 devices in a mesh: mut: 8 (over z, core), test: 4 (over y, x).
Axes of the slice: x: 2, y: 2, z: 4, core: 2. Of those that a mesh axis runs over, the one named last changes fastest.
Arguments:
- input_activation: bfloat16 [128, 28, 1024], P(('mut', 'test')), may hold values from -18 to 18
- ground_truth_class: int32 [128], replicated, may hold values from 0 to 999
- remaining_pictures: int32 [32, 56], P('mut', 'test'), may hold values from 0 to 31, as said below
- learned_narrowing_kernel: bfloat16 [1024, 256], replicated, may hold values from -0.1875 to 0.1875
- learned_widening_kernel: bfloat16 [256, 1024], replicated, may hold values from -0.375 to 0.375
- narrowing_perturbation: bfloat16 [32, 1024, 256], P('mut', 'test'), may hold values from -0.09375 to 0.09375
- widening_perturbation: bfloat16 [32, 256, 1024], P('mut', None, 'test'), may hold values from -0.1875 to 0.1875
- perturbation_strength: float32 [32, 2], P('mut'), may hold values from 0.25 to 2
- readout_matrix: bfloat16 [1024, 1000], replicated, may hold values from -1 to 1
Outputs:
- kill: float32 [32, 2, 56], P('mut', None, 'test')
Inputs may be any that keep to these rules, and one draw needn't show every extreme that they name: `remaining_pictures`: entry t * 14 + j of a mutant's row names an image of test shard t; image i of a shard lies on the device at mut index i // 4. Among the entries of one mut index's 4 mutants in one test shard, at most 10 lie on any one device's images, and some device takes exactly 10.
All inputs are finite; a program needn't handle non-finite values.
Results may differ from a plain program's by a relative error of at most 0.0003.
Values may be sent and summed in bfloat16 or wider, within the bound.
A program may use at most 64 MiB of HBM per device.

v0:
```python
import jax
import jax.numpy as jnp
from jax import lax
from jax.sharding import PartitionSpec as P


def on_device(
    input_activation,
    ground_truth_class,
    remaining_pictures,
    learned_narrowing_kernel,
    learned_widening_kernel,
    narrowing_perturbation,
    widening_perturbation,
    perturbation_strength,
    readout_matrix,
):
    n_test = lax.axis_size("test")
    variants_per_processor, remaining_flags = remaining_pictures.shape
    img_dev = input_activation.shape[0]
    steps = perturbation_strength.shape[1]
    width = learned_narrowing_kernel.shape[1]
    full_first, full_last = (
        lax.all_gather(narrowing_perturbation, "test", axis=1, tiled=True),
        lax.all_gather(widening_perturbation, "test", axis=2, tiled=True),
    )
    wanted_entries_sequence = remaining_pictures.reshape(-1)
    shard_index = lax.axis_index("test")
    whole = (
        wanted_entries_sequence // img_dev * n_test + shard_index
    ) * img_dev + wanted_entries_sequence % img_dev
    target_class_slice_full = jnp.take(ground_truth_class, whole)
    shard_images = lax.all_gather(input_activation, "mut", axis=0, tiled=True)
    selected_entries = jnp.take(shard_images, wanted_entries_sequence, axis=0)
    column = jnp.arange(readout_matrix.shape[1], dtype=jnp.int32)
    results = []
    for variant_member in range(variants_per_processor):
        bottleneck_unit = selected_entries[
            variant_member * remaining_flags : (variant_member + 1) * remaining_flags
        ]
        rows = bottleneck_unit.reshape(-1, bottleneck_unit.shape[2])
        target_class_slice = target_class_slice_full[
            variant_member * remaining_flags : (variant_member + 1) * remaining_flags
        ]
        first_list = []
        for step in range(steps):
            first_list.append(
                (
                    learned_narrowing_kernel.astype(jnp.float32)
                    + perturbation_strength[variant_member, step]
                    * full_first[variant_member].astype(jnp.float32)
                ).astype(jnp.bfloat16)
            )
        stacked_first = jnp.concatenate(first_list, axis=1)
        hidden_all = jnp.maximum(
            jnp.dot(rows, stacked_first, preferred_element_type=jnp.float32), 0.0
        ).astype(jnp.bfloat16)
        kills = []
        for step in range(steps):
            w_last = (
                learned_widening_kernel.astype(jnp.float32)
                + perturbation_strength[variant_member, step]
                * full_last[variant_member].astype(jnp.float32)
            ).astype(jnp.bfloat16)
            hidden = hidden_all[:, step * width : (step + 1) * width]
            out_rows = jnp.maximum(
                jnp.dot(hidden, w_last, preferred_element_type=jnp.float32)
                + rows.astype(jnp.float32),
                0.0,
            )
            pooled = jnp.mean(out_rows.reshape(bottleneck_unit.shape), axis=1).astype(jnp.bfloat16)
            logits = jnp.dot(pooled, readout_matrix, preferred_element_type=jnp.float32)
            top = jnp.max(logits, axis=1, keepdims=True)
            total = top[:, 0] + jnp.log(jnp.sum(jnp.exp(logits - top), axis=1))
            chosen = jnp.sum(
                jnp.where(column[None, :] == target_class_slice[:, None], logits, 0.0), axis=1
            )
            kills.append(total - chosen)
        results.append(jnp.stack(kills))
    return jnp.stack(results)


def solution(mesh):
    return jax.shard_map(
        on_device,
        mesh=mesh,
        in_specs=(
            P(("mut", "test"), None, None),
            P(),
            P("mut", "test"),
            P(),
            P(),
            P("mut", "test", None),
            P("mut", None, "test"),
            P("mut", None),
            P(),
        ),
        out_specs=P("mut", None, "test"),
        check_vma=False,
    )
```

profile of v0, /device:TPU:0, one launch (start us, length us, event | category | flops | bytes accessed | tf_op | source)
XLA Modules:
  0.0 199.8 jit_solution(2361325858595942928)
XLA Ops:
  7.3 1.7 copy.15
  9.8 0.8 reshape.435
  10.6 0.8 reshape.436
  11.4 0.8 gather_fusion.1
  13.0 34.4 %all-gather.6.cloned.1.call-done = bf16[4,1024,256]{2,1,0:T(8,128)(2,1)} async-done(((bf16[4,256,256]{2,1,0:T(8,128)(2,1)}), bf16[4,1024,256]{2,1,0:T(8,128)(2,1)}) %all-gather.6.cloned.1.call-update) | async-done | bytes 2097168 | tf_op jit(solution)/shard_map/all_gather | solution.py:24
  47.3 9.4 %fusion.28 = (bf16[1024,256]{1,0:T(8,128)(2,1)}, bf16[1024,256]{1,0:T(8,128)(2,1)}, bf16[1024,256]{1,0:T(8,128)(2,1)}, bf16[1024,256]{1,0:T(8,128)(2,1)}, bf16[1...) fusion(bf16[1024,256]{1,0:T(8,128)(2,1)S(1)} %copy-done.7, ...), kind=kLoop, calls=%fused_computation.75 | loop fusion | flops 7602176 | bytes 6815776 | tf_op jit(solution)/shard_map/convert_element_type | solution.py:52
  56.7 21.3 %all-gather.4.cloned.1.call-done = bf16[32,28,1024]{2,1,0:T(8,128)(2,1)} async-done(((bf16[4,28,1024]{2,1,0:T(8,128)(2,1)}), bf16[32,28,1024]{2,1,0:T(8,128)(2,1)}) %all-gather.4.cloned.1.call-update) | async-done | bytes 1835024 | tf_op jit(solution)/shard_map/all_gather | solution.py:33
  78.1 4.4 %gather_fusion = bf16[56,28,1024]{2,1,0:T(8,128)(2,1)} fusion(bf16[32,28,1024]{2,1,0:T(8,128)(2,1)} %all-gather.4.cloned.1.call-done, s32[1024]{0:T(1024)S(1)} %pad_clamp_fusion.1), kind=kCustom, calls=%fused_computation | custom fusion | bytes 6422752 | tf_op jit(solution)/shard_map/jit(_take)/gather | solution.py:34
  82.4 2.4 %broadcast_select_fusion = bf16[56,28,1024]{2,1,0:T(8,128)(2,1)S(1)} fusion(bf16[56,28,1024]{2,1,0:T(8,128)(2,1)} %gather_fusion, pred[56]{0:T(512)(128)(4,1)S(1)} %compare_and_fusion), kind=kLoop, calls=%fused_computation.2 | loop fusion | flops 1605632 | bytes 6422584 | tf_op jit(solution)/shard_map/jit(_take)/select_n | solution.py:34
  84.9 2.0 fusion.120
  86.8 1.3 reshape.437
  88.1 2.2 %reshape.446 = bf16[392,1024]{1,0:T(8,128)(2,1)} reshape(bf16[14,28,1024]{2,1,0:T(8,128)(2,1)} %get-tuple-element.22) | data formatting | bytes 1605632 | tf_op jit(solution)/shard_map/reshape | solution.py:41
  90.3 2.1 %reshape.443 = bf16[392,1024]{1,0:T(8,128)(2,1)} reshape(bf16[14,28,1024]{2,1,0:T(8,128)(2,1)} %get-tuple-element.23) | data formatting | bytes 1605632 | tf_op jit(solution)/shard_map/reshape | solution.py:41
  92.4 2.1 %reshape.440 = bf16[392,1024]{1,0:T(8,128)(2,1)} reshape(bf16[14,28,1024]{2,1,0:T(8,128)(2,1)} %get-tuple-element.24) | data formatting | bytes 1605632 | tf_op jit(solution)/shard_map/reshape | solution.py:41
  94.5 2.9 %fusion.11 = bf16[392,512]{1,0:T(8,128)(2,1)} fusion(bf16[392,1024]{1,0:T(8,128)(2,1)} %reshape.446, bf16[1024,256]{1,0:T(8,128)(2,1)} %get-tuple-element.32, bf16[1024,256]{1,0:T(8,128)(2,1)} %get-tuple-element.31), kind=kOutput, calls=%fused_computation.58 | convolution fusion | flops 413540352 | bytes 2252800 | tf_op jit(solution)/shard_map/dot_general | solution.py:56
  97.4 17.2 %all-gather.8.cloned.1.call-done = bf16[4,256,1024]{2,1,0:T(8,128)(2,1)} async-done(((bf16[4,256,256]{2,1,0:T(8,128)(2,1)}), bf16[4,256,1024]{2,1,0:T(8,128)(2,1)}) %all-gather.8.cloned.1.call-update) | async-done | bytes 2097168 | tf_op jit(solution)/shard_map/all_gather | solution.py:25
  114.6 3.6 %fusion.7 = f32[392,1024]{1,0:T(8,128)} fusion(bf16[392,1024]{1,0:T(8,128)(2,1)} %reshape.446, bf16[256,1024]{1,0:T(8,128)(2,1)S(1)} %copy-done.2, f32[]{:T(128)} %bitcast.31, bf16[4,256,1024]{2,1,0:T(8,128)(2,1)} %all-gather.8.cloned.1.call-done, bf16[392,512]{1,0:T(8,128)(2,1)} %fusion.11), kind=kOutput, calls=%fused_computation.34 | convolution fusion | flops 208035840 | bytes 3658240 | tf_op jit(solution)/shard_map/dot_general | solution.py:67
  118.2 2.6 %reshape.448 = f32[14,28,1024]{2,1,0:T(8,128)} reshape(f32[392,1024]{1,0:T(8,128)} %fusion.7) | data formatting | bytes 3211264 | tf_op jit(solution)/shard_map/reshape | solution.py:71
  120.9 3.5 %fusion.6 = f32[392,1024]{1,0:T(8,128)} fusion(bf16[392,1024]{1,0:T(8,128)(2,1)} %reshape.446, bf16[256,1024]{1,0:T(8,128)(2,1)S(1)} %copy-done.2, f32[]{:T(128)} %bitcast.29, bf16[4,256,1024]{2,1,0:T(8,128)(2,1)} %all-gather.8.cloned.1.call-done, bf16[392,512]{1,0:T(8,128)(2,1)} %fusion.11), kind=kOutput, calls=%fused_computation.33 | convolution fusion | flops 208035840 | bytes 3658240 | tf_op jit(solution)/shard_map/dot_general | solution.py:67
  124.4 2.7 %reshape.447 = f32[14,28,1024]{2,1,0:T(8,128)} reshape(f32[392,1024]{1,0:T(8,128)} %fusion.6) | data formatting | bytes 3211264 | tf_op jit(solution)/shard_map/reshape | solution.py:71
  127.1 1.8 reduce_sum.237
  128.9 1.8 reduce_sum.234
  130.7 1.4 fusion.124
  132.1 1.4 fusion.123
  134.8 3.3 %fusion.5 = f32[392,1024]{1,0:T(8,128)} fusion(bf16[392,1024]{1,0:T(8,128)(2,1)S(1)} %copy-done.5, bf16[256,1024]{1,0:T(8,128)(2,1)S(1)} %copy-done.2, f32[]{:T(128)} %bitcast.22, bf16[4,256,1024]{2,1,0:T(8,128)(2,1)} %all-gather.8.cloned.1.call-done, bf16[392,512]{1,0:T(8,128)(2,1)S(1)} %fusion.10), kind=kOutput, calls=%fused_computation.32 | convolution fusion | flops 208035840 | bytes 3658240 | tf_op jit(solution)/shard_map/dot_general | solution.py:67
  138.1 2.7 %reshape.445 = f32[14,28,1024]{2,1,0:T(8,128)} reshape(f32[392,1024]{1,0:T(8,128)} %fusion.5) | data formatting | bytes 3211264 | tf_op jit(solution)/shard_map/reshape | solution.py:71
  140.8 1.8 reduce_sum.231
  142.6 1.4 fusion.126
  144.0 3.3 %fusion.4 = f32[392,1024]{1,0:T(8,128)} fusion(bf16[392,1024]{1,0:T(8,128)(2,1)S(1)} %copy-done.6, bf16[256,1024]{1,0:T(8,128)(2,1)S(1)} %copy-done.2, f32[]{:T(128)} %bitcast.20, bf16[4,256,1024]{2,1,0:T(8,128)(2,1)} %all-gather.8.cloned.1.call-done, bf16[392,512]{1,0:T(8,128)(2,1)S(1)} %copy-done.17), kind=kOutput, calls=%fused_computation.31 | convolution fusion | flops 208035840 | bytes 3658240 | tf_op jit(solution)/shard_map/dot_general | solution.py:67
  147.2 2.7 %reshape.444 = f32[14,28,1024]{2,1,0:T(8,128)} reshape(f32[392,1024]{1,0:T(8,128)} %fusion.4) | data formatting | bytes 3211264 | tf_op jit(solution)/shard_map/reshape | solution.py:71
  149.9 1.8 reduce_sum.228
  151.7 1.4 fusion.125
  154.5 3.4 %fusion.3 = f32[392,1024]{1,0:T(8,128)} fusion(bf16[392,1024]{1,0:T(8,128)(2,1)S(1)} %copy-done.3, bf16[256,1024]{1,0:T(8,128)(2,1)S(1)} %copy-done.2, f32[]{:T(128)} %bitcast.13, bf16[4,256,1024]{2,1,0:T(8,128)(2,1)} %all-gather.8.cloned.1.call-done, bf16[392,512]{1,0:T(8,128)(2,1)S(1)} %fusion.9), kind=kOutput, calls=%fused_computation.30 | convolution fusion | flops 208035840 | bytes 3658240 | tf_op jit(solution)/shard_map/dot_general | solution.py:67
  157.8 2.7 %reshape.442 = f32[14,28,1024]{2,1,0:T(8,128)} reshape(f32[392,1024]{1,0:T(8,128)} %fusion.3) | data formatting | bytes 3211264 | tf_op jit(solution)/shard_map/reshape | solution.py:71
  160.5 1.8 reduce_sum.225
  162.3 0.8 fusion.128
  163.6 3.3 %fusion.2 = f32[392,1024]{1,0:T(8,128)} fusion(bf16[392,1024]{1,0:T(8,128)(2,1)S(1)} %copy-done.4, bf16[256,1024]{1,0:T(8,128)(2,1)S(1)} %copy-done.2, f32[]{:T(128)} %bitcast.11, bf16[4,256,1024]{2,1,0:T(8,128)(2,1)} %all-gather.8.cloned.1.call-done, bf16[392,512]{1,0:T(8,128)(2,1)S(1)} %copy-done.19), kind=kOutput, calls=%fused_computation.29 | convolution fusion | flops 208035840 | bytes 3658240 | tf_op jit(solution)/shard_map/dot_general | solution.py:67
  166.9 2.7 %reshape.441 = f32[14,28,1024]{2,1,0:T(8,128)} reshape(f32[392,1024]{1,0:T(8,128)} %fusion.2) | data formatting | bytes 3211264 | tf_op jit(solution)/shard_map/reshape | solution.py:71
  169.5 1.8 reduce_sum.222
  171.3 1.4 fusion.127
  174.1 3.3 %fusion = f32[392,1024]{1,0:T(8,128)} fusion(bf16[392,1024]{1,0:T(8,128)(2,1)S(1)} %reshape.437, bf16[256,1024]{1,0:T(8,128)(2,1)S(1)} %copy-done.2, f32[]{:T(128)} %bitcast.1, bf16[4,256,1024]{2,1,0:T(8,128)(2,1)} %all-gather.8.cloned.1.call-done, bf16[392,512]{1,0:T(8,128)(2,1)S(1)} %fusion.8), kind=kOutput, calls=%fused_computation.27 | convolution fusion | flops 208035840 | bytes 3658240 | tf_op jit(solution)/shard_map/dot_general | solution.py:67
  177.4 2.6 %reshape.438 = f32[14,28,1024]{2,1,0:T(8,128)} reshape(f32[392,1024]{1,0:T(8,128)} %fusion) | data formatting | bytes 3211264 | tf_op jit(solution)/shard_map/reshape | solution.py:71
  180.1 1.8 reduce_sum.216
  181.8 1.4 fusion.129
  183.2 3.3 %fusion.1 = f32[392,1024]{1,0:T(8,128)} fusion(bf16[392,1024]{1,0:T(8,128)(2,1)S(1)} %reshape.437, bf16[256,1024]{1,0:T(8,128)(2,1)S(1)} %copy-done.2, f32[]{:T(128)} %bitcast.3, bf16[4,256,1024]{2,1,0:T(8,128)(2,1)} %all-gather.8.cloned.1.call-done, bf16[392,512]{1,0:T(8,128)(2,1)S(1)} %copy-done.15), kind=kOutput, calls=%fused_computation.28 | convolution fusion | flops 208035840 | bytes 3658240 | tf_op jit(solution)/shard_map/dot_general | solution.py:67
  186.5 2.6 %reshape.439 = f32[14,28,1024]{2,1,0:T(8,128)} reshape(f32[392,1024]{1,0:T(8,128)} %fusion.1) | data formatting | bytes 3211264 | tf_op jit(solution)/shard_map/reshape | solution.py:71
  189.2 1.8 reduce_sum.219
  191.0 0.8 fusion.130
  (85 shorter events, 8.2 us)
Async XLA Ops:
  6.5 124.1 %copy-start = (bf16[1024,1000]{0,1:T(8,128)(2,1)S(1)}, bf16[1024,1000]{0,1:T(8,128)(2,1)}, u32[]{:S(2)}) copy-start(bf16[1024,1000]{0,1:T(8,128)(2,1)} %param.17) | copy-start | bytes 6144004
  6.5 4.8 %copy-start.1 = (s32[128]{0:T(128)S(1)}, s32[128]{0:T(128)}, u32[]{:S(2)}) copy-start(s32[128]{0:T(128)} %param.10) | copy-start | bytes 1540
  6.5 5.6 %copy-start.26 = (f32[4,2]{0,1:T(2,128)S(1)}, f32[4,2]{0,1:T(2,128)}, u32[]{:S(2)}) copy-start(f32[4,2]{0,1:T(2,128)} %param.16) | copy-start | bytes 100
  6.5 40.8 %copy-start.7 = (bf16[1024,256]{1,0:T(8,128)(2,1)S(1)}, bf16[1024,256]{1,0:T(8,128)(2,1)}, u32[]{:S(2)}) copy-start(bf16[1024,256]{1,0:T(8,128)(2,1)} %param.12) | copy-start | bytes 1572868
  6.5 40.8 %all-gather.6.cloned.1.call-start = ((), (), s32[]{:S(2)}) async-start(), calls=%async_computation.1 | async-start | bytes 2621440 | tf_op jit(solution)/shard_map/all_gather | solution.py:24
  7.3 70.8 %all-gather.4.cloned.1.call-start = ((), (), s32[]{:S(2)}) async-start(), calls=%async_computation | async-start | bytes 2359296 | tf_op jit(solution)/shard_map/all_gather | solution.py:33
  9.1 105.5 %all-gather.8.cloned.1.call-start = ((), (), s32[]{:S(2)}) async-start(), calls=%async_computation.2 | async-start | bytes 2621440 | tf_op jit(solution)/shard_map/all_gather | solution.py:25
  94.5 20.1 %copy-start.2 = (bf16[256,1024]{1,0:T(8,128)(2,1)S(1)}, bf16[256,1024]{1,0:T(8,128)(2,1)}, u32[]{:S(2)}) copy-start(bf16[256,1024]{1,0:T(8,128)(2,1)} %param.13) | copy-start | bytes 1572868
  130.7 2.8 %copy-start.5 = (bf16[392,1024]{1,0:T(8,128)(2,1)S(1)}, bf16[392,1024]{1,0:T(8,128)(2,1)}, u32[]{:S(2)}) copy-start(bf16[392,1024]{1,0:T(8,128)(2,1)} %reshape.443) | copy-start | bytes 2408452
  130.7 2.8 %copy-start.12 = (bf16[1024,256]{1,0:T(8,128)(2,1)S(1)}, bf16[1024,256]{1,0:T(8,128)(2,1)}, u32[]{:S(2)}) copy-start(bf16[1024,256]{1,0:T(8,128)(2,1)} %get-tuple-element.29) | copy-start | bytes 1572868
  130.7 2.8 %copy-start.13 = (bf16[1024,256]{1,0:T(8,128)(2,1)S(1)}, bf16[1024,256]{1,0:T(8,128)(2,1)}, u32[]{:S(2)}) copy-start(bf16[1024,256]{1,0:T(8,128)(2,1)} %get-tuple-element.30) | copy-start | bytes 1572868
  134.1 0.8 copy-start.16
  142.6 1.4 copy-start.6
  142.6 1.4 copy-start.17
  151.7 1.4 copy-start.3
  151.7 1.4 copy-start.10
  151.7 1.4 copy-start.11
  153.7 0.7 copy-start.18
  162.3 1.1 copy-start.4
  162.3 1.2 copy-start.19
  171.3 1.4 copy-start.8
  171.3 1.4 copy-start.9
  173.3 0.8 copy-start.14
  181.8 1.4 copy-start.15
  189.1 2.6 %copy-start.20 = (f32[14,1000]{1,0:T(8,128)S(1)}, f32[14,1000]{1,0:T(8,128)}, u32[]{:S(2)}) copy-start(f32[14,1000]{1,0:T(8,128)} %get-tuple-element.58) | copy-start | bytes 168004
  189.1 2.6 %copy-start.21 = (f32[14,1000]{1,0:T(8,128)S(1)}, f32[14,1000]{1,0:T(8,128)}, u32[]{:S(2)}) copy-start(f32[14,1000]{1,0:T(8,128)} %get-tuple-element.56) | copy-start | bytes 168004
  189.1 2.6 %copy-start.23 = (f32[14,1000]{1,0:T(8,128)S(1)}, f32[14,1000]{1,0:T(8,128)}, u32[]{:S(2)}) copy-start(f32[14,1000]{1,0:T(8,128)} %get-tuple-element.62) | copy-start | bytes 168004
  189.1 2.7 %copy-start.25 = (f32[14,1000]{1,0:T(8,128)S(1)}, f32[14,1000]{1,0:T(8,128)}, u32[]{:S(2)}) copy-start(f32[14,1000]{1,0:T(8,128)} %get-tuple-element.60) | copy-start | bytes 168004
  189.1 3.1 %copy-start.22 = (f32[14,1000]{1,0:T(8,128)S(1)}, f32[14,1000]{1,0:T(8,128)}, u32[]{:S(2)}) copy-start(f32[14,1000]{1,0:T(8,128)} %get-tuple-element.64) | copy-start | bytes 168004
  189.2 3.1 %copy-start.24 = (f32[14,1000]{1,0:T(8,128)S(1)}, f32[14,1000]{1,0:T(8,128)}, u32[]{:S(2)}) copy-start(f32[14,1000]{1,0:T(8,128)} %get-tuple-element.68) | copy-start | bytes 168004
Sparse Core Ops, SparseCore 0:
  9.2 38.0 all-gather.5
  48.9 29.0 all-gather.3
  79.9 34.6 all-gather.7
where the time goes:
time: 201 us; the launch traced here: 200 us
  waiting for transfers between devices  74.2 us (37%)
  local copies, waits for them, and re-layouts  42.9 us (21%)
  matrix products  41.5 us (21%)
  other arithmetic  27.5 us (14%)
  between operations  13.6 us (7%)
    all_gather x1, waiting for transfers between devices, on_device(): lax.all_gather(narrowing_perturbation, 'test', axis=1, tiled=True)  34.4 us
    dot_general x8, matrix products, on_device(): jnp.dot(hidden, w_last, preferred_element_type=jnp.float32)  27 us
    all_gather x1, waiting for transfers between devices, on_device(): shard_images = lax.all_gather(input_activation, 'mut', axis=0, tiled=True)  21.3 us
    reshape x8, local copies, waits for them, and re-layouts, on_device(): out_rows.reshape(bottleneck_unit.shape)  21.3 us
    all_gather x1, waiting for transfers between devices, on_device(): lax.all_gather(widening_perturbation, 'test', axis=2, tiled=True)  17.2 us
    reduce_sum x8, other arithmetic, on_device(): jnp.mean(out_rows.reshape(bottleneck_unit.shape), axis=1)  14.3 us
    dot_general x8, matrix products, on_device(): logits = jnp.dot(pooled, readout_matrix, preferred_element_type=jnp.float32)  9.83 us
    convert_element_type x1, other arithmetic, on_device(): first_list.append((learned_narrowing_kernel.astype(jnp.float32) + perturb...  9.39 us
  transfers between devices with their start and end apart: 3, of which 3 were waited for; matrix products, arithmetic and copies ran while one was open for 17% of the time, Pallas kernels for 0%

commit v1 on v0

v1 whole, which is shorter than its diff:
```python
import functools

import jax
import jax.numpy as jnp
from jax import lax
from jax.experimental import pallas as pl
from jax.experimental.pallas import tpu as pltpu
from jax.sharding import PartitionSpec as P

MESH = pl.DeviceIdType.MESH
F32, BF16 = jnp.float32, jnp.bfloat16


def round_up(value, unit):
    return (value + unit - 1) // unit * unit


def kernel(
    n_mut,
    n_test,
    left_ref,
    strength_ref,
    label_ref,
    x_ref,
    d1_ref,
    d2_ref,
    w1_ref,
    w2_ref,
    readout_ref,
    kill_ref,
    images,
    d1_all,
    d2_all,
    w1,
    w2,
    readout,
    rows,
    w1_step,
    pooled,
    labels,
    local_sem,
    x_send,
    x_recv,
    sib_send,
    sib_recv,
    d_send,
    d_recv,
):
    img_dev, pix, width = x_ref.shape
    slot = images.shape[1]
    n_var, surv = left_ref.shape
    steps = strength_ref.shape[1]
    block = d1_ref.shape[1]
    narrow = d1_ref.shape[2]
    padded = pooled.shape[1]
    m, t = lax.axis_index("mut"), lax.axis_index("test")
    chips = n_mut // 2
    sibling = m + 1 - 2 * (m % 2)
    far = [(m + 2 * k) % n_mut for k in range(1, chips)]
    far_from = [(m + n_mut - 2 * k) % n_mut for k in range(1, chips)]
    square = n_test == 4
    if square:
        across, along = t + 1 - 2 * (t % 2), (t + 2) % 4
        near = [across, along]
        origin = [across, along, 3 - t]
    else:
        near = [(t + k) % n_test for k in range(1, n_test)]
        origin = [(t + n_test - k) % n_test for k in range(1, n_test)]

    local = [
        pltpu.make_async_copy(w1_ref, w1, local_sem.at[0]),
        pltpu.make_async_copy(w2_ref, w2, local_sem.at[1]),
        pltpu.make_async_copy(readout_ref, readout, local_sem.at[2]),
        pltpu.make_async_copy(d1_ref, d1_all.at[:, t], local_sem.at[3]),
        pltpu.make_async_copy(d2_ref, d2_all.at[:, t], local_sem.at[4]),
    ]

    barrier = pltpu.get_barrier_semaphore()
    for peer in [sibling] + far:
        pl.semaphore_signal(barrier, inc=1, device_id=(peer, t), device_id_type=MESH)
    for peer in near:
        pl.semaphore_signal(barrier, inc=1, device_id=(m, peer), device_id_type=MESH)
    for copy in local:
        copy.start()
    images[pl.ds(m * img_dev, img_dev)] = jnp.concatenate(
        [x_ref[...], jnp.zeros((img_dev, slot - pix, width), BF16)], axis=1
    )
    pl.semaphore_wait(barrier, 1 + len(far) + len(near))

    def x_copy(source, send, recv, target):
        view = images.at[pl.ds(source * img_dev, img_dev)]
        return pltpu.make_async_remote_copy(
            view, view, send, recv, device_id=(target, t), device_id_type=MESH
        )

    def own_copy(which, i, place):
        ref, full = ((d1_ref, d1_all), (d2_ref, d2_all))[which]
        return pltpu.make_async_remote_copy(
            ref.at[i],
            full.at[i, t],
            d_send.at[which, i, place],
            d_recv.at[which, i, place],
            device_id=(m, near[place]),
            device_id_type=MESH,
        )

    def held_copy(which, i, place, target):
        view = (d1_all, d2_all)[which].at[i, origin[place]]
        return pltpu.make_async_remote_copy(
            view,
            view,
            d_send.at[which, i, 2],
            d_recv.at[which, i, 2],
            device_id=(m, target),
            device_id_type=MESH,
        )

    def arrived(which, i, place):
        view = (d1_all, d2_all)[which].at[i, origin[place]]
        pltpu.make_async_remote_copy(
            view,
            view,
            d_send.at[which, i, place],
            d_recv.at[which, i, place],
            device_id=(m, near[0]),
            device_id_type=MESH,
        ).wait_recv()

    def send_own(i):
        for which in range(2):
            for place in range(len(near)):
                own_copy(which, i, place).start()

    def pass_on(i):
        if square:
            arrived(0, i, 0)
            held_copy(0, i, 0, along).start()
            arrived(1, i, 1)
            held_copy(1, i, 1, across).start()

    x_out = [x_copy(m, x_send.at[k], x_recv.at[k], far[k]) for k in range(chips - 1)]
    sib_out = [x_copy(m, sib_send.at[0], sib_recv.at[0], sibling)]
    for copy in x_out:
        copy.start()
    send_own(0)
    send_own(1)
    sib_out[0].start()
    pass_on(0)
    for i in range(2, n_var):
        send_own(i)
    pass_on(1)
    for k in range(chips - 1):
        x_copy(far_from[k], x_send.at[k], x_recv.at[k], far[k]).wait_recv()
        copy = x_copy(far_from[k], sib_send.at[k + 1], sib_recv.at[k + 1], sibling)
        copy.start()
        sib_out.append(copy)
    sib_from = [sibling] + [(sibling + n_mut - 2 * k) % n_mut for k in range(1, chips)]
    for k in range(chips):
        x_copy(sib_from[k], sib_send.at[k], sib_recv.at[k], sibling).wait_recv()
    for copy in local:
        copy.wait()

    def variant(i, carry):
        for place in range(len(origin)):
            for which in range(2):
                if not (square and place == which):
                    arrived(which, i, place)
        for j in range(surv):
            entry = left_ref[i, j]
            rows[pl.ds(j * slot, slot), :] = images[entry]
            number = (entry // img_dev * n_test + t) * img_dev + entry % img_dev
            labels[i, pl.ds(j, 1), :] = jnp.full((1, 128), label_ref[number], jnp.int32)
        for step in range(steps):
            strength = strength_ref[i, step]
            for part in range(n_test):
                span = pl.ds(part * block, block)
                w1_step[span, :] = (
                    w1[span, :].astype(F32) + strength * d1_all[i, part].astype(F32)
                ).astype(BF16)
            hidden = jnp.maximum(
                jnp.dot(rows[...], w1_step[...], preferred_element_type=F32), 0.0
            ).astype(BF16)
            for part in range(n_test):
                span = pl.ds(part * block, block)
                w2_step = (
                    w2[:, span].astype(F32) + strength * d2_all[i, part].astype(F32)
                ).astype(BF16)
                out = jnp.maximum(
                    jnp.dot(hidden, w2_step, preferred_element_type=F32)
                    + rows[:, span].astype(F32),
                    0.0,
                )
                mean = jnp.sum(out.reshape(surv, slot, block), axis=1) * (1.0 / pix)
                pooled[i * steps + step, :, span] = jnp.concatenate(
                    [mean, jnp.zeros((padded - surv, block), F32)], axis=0
                ).astype(BF16)
        if square:

            @pl.when(i + 2 < n_var)
            def _():
                pass_on(i + 2)

        return carry

    lax.fori_loop(0, n_var, variant, 0)

    count = n_var * steps * padded
    logits = jnp.dot(
        pooled[...].reshape(count, width), readout[...], preferred_element_type=F32
    )
    classes = logits.shape[1]
    top = jnp.max(logits, axis=1, keepdims=True)
    total = top + jnp.log(jnp.sum(jnp.exp(logits - top), axis=1, keepdims=True))
    wanted = jnp.concatenate(
        [labels[i // steps][:, 0:1] for i in range(n_var * steps)], axis=0
    )
    column = lax.broadcasted_iota(jnp.int32, (count, classes), 1)
    chosen = jnp.sum(jnp.where(column == wanted, logits, 0.0), axis=1, keepdims=True)
    kill = total - chosen
    row = lax.broadcasted_iota(jnp.int32, (count, 128), 0) % padded
    lane = lax.broadcasted_iota(jnp.int32, (count, 128), 1)
    spread = jnp.sum(
        jnp.where(row == lane, kill, 0.0).reshape(n_var * steps, padded, 128), axis=1
    )
    for i in range(n_var):
        kill_ref[i] = spread[i * steps : (i + 1) * steps, :surv]

    for copy in x_out + sib_out:
        copy.wait_send()

    def drain(i, carry):
        for which in range(2):
            for place in range(len(near)):
                own_copy(which, i, place).wait_send()
        if square:
            held_copy(0, i, 0, along).wait_send()
            held_copy(1, i, 1, across).wait_send()
        return carry

    lax.fori_loop(0, n_var, drain, 0)


def solution(mesh):
    n_mut, n_test = mesh.shape["mut"], mesh.shape["test"]

    def on_device(x, label, left, w1, w2, d1, d2, strength, readout):
        img_dev, pix, width = x.shape
        n_var, surv = left.shape
        steps = strength.shape[1]
        block, narrow = d1.shape[1], d1.shape[2]
        slot = round_up(pix, 16)
        padded = round_up(surv, 16)
        dma = pltpu.SemaphoreType.DMA
        places = max(3, n_test - 1)
        chips = n_mut // 2
        smem = pl.BlockSpec(memory_space=pltpu.SMEM)
        vmem = pl.BlockSpec(memory_space=pltpu.VMEM)
        anywhere = pl.BlockSpec(memory_space=pl.ANY)
        macs = n_var * steps * surv * slot * width * narrow * 2
        return pl.pallas_call(
            functools.partial(kernel, n_mut, n_test),
            out_shape=jax.ShapeDtypeStruct((n_var, steps, surv), F32),
            in_specs=[smem, smem, smem, vmem] + [anywhere] * 5,
            out_specs=vmem,
            scratch_shapes=[
                pltpu.VMEM((n_mut * img_dev, slot, width), BF16),
                pltpu.VMEM((n_var, n_test, block, narrow), BF16),
                pltpu.VMEM((n_var, n_test, narrow, block), BF16),
                pltpu.VMEM(w1.shape, BF16),
                pltpu.VMEM(w2.shape, BF16),
                pltpu.VMEM(readout.shape, BF16),
                pltpu.VMEM((surv * slot, width), BF16),
                pltpu.VMEM((width, narrow), BF16),
                pltpu.VMEM((n_var * steps, padded, width), BF16),
                pltpu.VMEM((n_var, padded, 128), jnp.int32),
                dma((5,)),
                dma((chips,)),
                dma((chips,)),
                dma((chips,)),
                dma((chips,)),
                dma((2, n_var, places)),
                dma((2, n_var, places)),
            ],
            compiler_params=pltpu.CompilerParams(
                collective_id=0, has_side_effects=True, vmem_limit_bytes=48 * 2**20
            ),
            cost_estimate=pl.CostEstimate(
                flops=2 * macs, bytes_accessed=8 * 2**20, transcendentals=0
            ),
        )(left, strength, label, x, d1, d2, w1, w2, readout)

    return jax.shard_map(
        on_device,
        mesh=mesh,
        in_specs=(
            P(("mut", "test"), None, None),
            P(),
            P("mut", "test"),
            P(),
            P(),
            P("mut", "test", None),
            P("mut", None, "test"),
            P("mut", None),
            P(),
        ),
        out_specs=P("mut", None, "test"),
        check_vma=False,
    )
```

time: 201 us -> 53.9 us (0.27)
  waiting for transfers between devices: 74.2 us -> 0 us
  Pallas kernels: 0 us -> 46.1 us
  matrix products: 41.5 us -> 0 us
  local copies, waits for them, and re-layouts: 42.9 us -> 7.4 us
  other arithmetic: 27.5 us -> 0 us
  between operations: 13.6 us -> 0.1 us
    all_gather x3 -> x0, waiting for transfers between devices: 72.9 us -> none  [the longest x1 34.4 us: on_device(): lax.all_gather(narrowing_perturbation, 'test', axis=1, tiled=True)]
    pallas_call x0 -> x1, Pallas kernels: none -> 46.1 us  [on_device(): pl.pallas_call(functools.partial(kernel, n_mut, n_test), out_shape=jax.Sh...]
    dot_general x20 -> x0, matrix products: 41.5 us -> none  [the longest x8 27 us: on_device(): jnp.dot(hidden, w_last, preferred_element_type=jnp.float32)]
    reshape x14 -> x0, local copies, waits for them, and re-layouts: 30.5 us -> none  [the longest x8 21.3 us: on_device(): out_rows.reshape(bottleneck_unit.shape)]
    reduce_sum x10 -> x0, other arithmetic: 14.9 us -> none  [the longest x8 14.3 us: on_device(): jnp.mean(out_rows.reshape(bottleneck_unit.shape), axis=1)]
    convert_element_type x1 -> x0, other arithmetic: 9.39 us -> none  [on_device(): first_list.append((learned_narrowing_kernel.astype(jnp.float32) + perturb...]
    gather x2 -> x0, local copies, waits for them, and re-layouts: 5.15 us -> none  [the longest x1 4.37 us: on_device(): selected_entries = jnp.take(shard_images, wanted_entries_sequence, axis=0)]
    unnamed x55 -> x16, local copies, waits for them, and re-layouts: 4.51 us -> 7.4 us
  transfers between devices with their start and end apart: 3 -> 0, of which waited for: 3 -> 0; matrix products, arithmetic and copies ran while one was open for 17% -> 0% of each run, Pallas kernels for 0% -> 0%
where the time goes in v1:
time: 53.9 us; the launch traced here: 53.6 us
  Pallas kernels  46.1 us (86%)
  local copies, waits for them, and re-layouts  7.4 us (14%)
    pallas_call x1, Pallas kernels, on_device(): pl.pallas_call(functools.partial(kernel, n_mut, n_test), out_shape=jax.Sh...  46.1 us
    unnamed x16, local copies, waits for them, and re-layouts  7.4 us

profile of v1, /device:TPU:0, one launch (start us, length us, event | category | flops | bytes accessed | tf_op | source)
XLA Modules:
  0.0 53.6 jit_solution(17713144816689939017)
XLA Ops:
  0.0 0.8 %copy.10.strength_ref = f32[4,2]{1,0:T(4,128)S(1)} copy(f32[4,2]{0,1:T(2,128)} %param.16) | data formatting | bytes 64 | tf_op args[7]
  0.8 1.0 %copy.11.x_ref = bf16[4,28,1024]{2,1,0:T(8,128)(2,1)S(1)} copy(bf16[4,28,1024]{2,0,1:T(4,128)(2,1)} %param.9) | data formatting | bytes 458752 | tf_op args[0]
  1.8 0.0 copy-start
  1.8 0.0 copy-start.1
  1.8 0.0 copy-start.4
  1.8 0.0 copy-start.5
  1.8 2.9 %copy.12.readout_ref = bf16[1024,1000]{1,0:T(8,128)(2,1)S(1)} copy(bf16[1024,1000]{0,1:T(8,128)(2,1)} %param.17) | data formatting | bytes 4096000 | tf_op args[8]
  4.8 0.0 copy-done
  4.8 0.0 copy-done.1
  4.8 0.0 copy-done.4
  4.8 0.0 copy-done.5
  4.8 0.0 copy-start.2
  4.8 1.0 %copy-done.2 = bf16[1024,256]{1,0:T(8,128)(2,1)S(1)} copy-done((bf16[1024,256]{1,0:T(8,128)(2,1)S(1)}, bf16[1024,256]{1,0:T(8,128)(2,1)}, u32[]{:S(2)}) %copy-start.2) | copy-done | bytes 524312
  5.9 0.0 copy-start.3
  5.9 1.0 %copy-done.3 = bf16[256,1024]{1,0:T(8,128)(2,1)S(1)} copy-done((bf16[256,1024]{1,0:T(8,128)(2,1)S(1)}, bf16[256,1024]{1,0:T(8,128)(2,1)}, u32[]{:S(2)}) %copy-start.3) | copy-done | bytes 524312
  6.9 46.1 %shard_map.91 = f32[4,2,14]{2,1,0:T(2,128)S(1)} custom-call(s32[4,14]{1,0:T(4,128)S(1)} %copy-done.4, f32[4,2]{1,0:T(4,128)S(1)} %copy.10.strength_ref, s32[128]{0:T(128)S(1)} %copy-done.5, bf16[4,28,1024]{2,1,0:T(8,128)(2,1)S(1)} %copy.11.x_ref, bf16[4,256,256]{2,1,0:T(8,128)(2,1)S(1)} %copy-done, bf16[4,256,256]{2,1,0:T(8,128)(2,1)S(1)} %copy-done.1, ...), custom_call_target="tpu_custom_call" | custom-call | flops 3758096384 | bytes 8388608 | tf_op jit(solution)/shard_map/pallas_call | solution.py:260
  53.0 0.6 %copy.14 = f32[4,2,14]{2,1,0:T(2,128)} copy(f32[4,2,14]{2,1,0:T(2,128)S(1)} %shard_map.91) | data formatting | bytes 896
Async XLA Ops:
  1.8 3.0 %copy-start = (bf16[4,256,256]{2,1,0:T(8,128)(2,1)S(1)}, bf16[4,256,256]{2,1,0:T(8,128)(2,1)}, u32[]{:S(2)}) copy-start(bf16[4,256,256]{2,1,0:T(8,128)(2,1)} %d1_ref.1) | copy-start | bytes 1572868
  1.8 3.0 %copy-start.1 = (bf16[4,256,256]{2,1,0:T(8,128)(2,1)S(1)}, bf16[4,256,256]{2,1,0:T(8,128)(2,1)}, u32[]{:S(2)}) copy-start(bf16[4,256,256]{2,1,0:T(8,128)(2,1)} %d2_ref.1) | copy-start | bytes 1572868
  1.8 3.0 %copy-start.4 = (s32[4,14]{1,0:T(4,128)S(1)}, s32[4,14]{1,0:T(4,128)}, u32[]{:S(2)}) copy-start(s32[4,14]{1,0:T(4,128)} %left_ref.1) | copy-start | bytes 676
  1.8 3.0 %copy-start.5 = (s32[128]{0:T(128)S(1)}, s32[128]{0:T(128)}, u32[]{:S(2)}) copy-start(s32[128]{0:T(128)} %label_ref.1) | copy-start | bytes 1540
  4.8 1.0 %copy-start.2 = (bf16[1024,256]{1,0:T(8,128)(2,1)S(1)}, bf16[1024,256]{1,0:T(8,128)(2,1)}, u32[]{:S(2)}) copy-start(bf16[1024,256]{1,0:T(8,128)(2,1)} %w1_ref.1) | copy-start | bytes 1572868
  5.9 1.0 %copy-start.3 = (bf16[256,1024]{1,0:T(8,128)(2,1)S(1)}, bf16[256,1024]{1,0:T(8,128)(2,1)}, u32[]{:S(2)}) copy-start(bf16[256,1024]{1,0:T(8,128)(2,1)} %w2_ref.1) | copy-start | bytes 1572868

commit v2 on v1

--- a/solution.py
+++ b/solution.py
@@ -46,18 +46,17 @@
     d_send,
     d_recv,
 ):
-    img_dev, pix, width = x_ref.shape
+    pix, img_dev, width = x_ref.shape
     slot = images.shape[1]
     n_var, surv = left_ref.shape
-    steps = strength_ref.shape[1]
+    steps = strength_ref.shape[0]
     block = d1_ref.shape[1]
     narrow = d1_ref.shape[2]
     padded = pooled.shape[1]
     m, t = lax.axis_index("mut"), lax.axis_index("test")
     chips = n_mut // 2
     sibling = m + 1 - 2 * (m % 2)
-    far = [(m + 2 * k) % n_mut for k in range(1, chips)]
-    far_from = [(m + n_mut - 2 * k) % n_mut for k in range(1, chips)]
+    chip = m // 2
     square = n_test == 4
     if square:
         across, along = t + 1 - 2 * (t % 2), (t + 2) % 4
@@ -67,6 +66,9 @@
         near = [(t + k) % n_test for k in range(1, n_test)]
         origin = [(t + n_test - k) % n_test for k in range(1, n_test)]
 
+    def reaches(sign, k):
+        return chip + k < chips if sign > 0 else chip >= k
+
     local = [
         pltpu.make_async_copy(w1_ref, w1, local_sem.at[0]),
         pltpu.make_async_copy(w2_ref, w2, local_sem.at[1]),
@@ -76,16 +78,26 @@
     ]
 
     barrier = pltpu.get_barrier_semaphore()
-    for peer in [sibling] + far:
-        pl.semaphore_signal(barrier, inc=1, device_id=(peer, t), device_id_type=MESH)
+    pl.semaphore_signal(barrier, inc=1, device_id=(sibling, t), device_id_type=MESH)
+    for sign in (1, -1):
+
+        @pl.when(reaches(sign, 1))
+        def _():
+            pl.semaphore_signal(
+                barrier, inc=1, device_id=(m + 2 * sign, t), device_id_type=MESH
+            )
+
     for peer in near:
         pl.semaphore_signal(barrier, inc=1, device_id=(m, peer), device_id_type=MESH)
     for copy in local:
         copy.start()
-    images[pl.ds(m * img_dev, img_dev)] = jnp.concatenate(
-        [x_ref[...], jnp.zeros((img_dev, slot - pix, width), BF16)], axis=1
-    )
-    pl.semaphore_wait(barrier, 1 + len(far) + len(near))
+    for j in range(img_dev):
+        images[m * img_dev + j] = jnp.concatenate(
+            [x_ref[:, j, :], jnp.zeros((slot - pix, width), BF16)], axis=0
+        )
+    below = (chip + chips - 1) // chips
+    above = (2 * chips - 2 - chip) // chips
+    pl.semaphore_wait(barrier, 1 + len(near) + below + above)
 
     def x_copy(source, send, recv, target):
         view = images.at[pl.ds(source * img_dev, img_dev)]
@@ -138,25 +150,66 @@
             arrived(1, i, 1)
             held_copy(1, i, 1, across).start()
 
-    x_out = [x_copy(m, x_send.at[k], x_recv.at[k], far[k]) for k in range(chips - 1)]
-    sib_out = [x_copy(m, sib_send.at[0], sib_recv.at[0], sibling)]
-    for copy in x_out:
-        copy.start()
+    def hop(sign, k):
+        way = (1 - sign) // 2
+        return x_copy(
+            m - 2 * sign * k, x_send.at[way, k], x_recv.at[way, k + 1], m + 2 * sign
+        )
+
+    def landed(sign, k):
+        way = (1 - sign) // 2
+        return x_copy(
+            m - 2 * sign * k, x_send.at[way, k], x_recv.at[way, k], m + 2 * sign
+        )
+
+    def hand_over(sign, k):
+        way = (1 - sign) // 2
+        return x_copy(
+            m - 2 * sign * k, sib_send.at[way, k], sib_recv.at[way, k], sibling
+        )
+
+    def handed(sign, k):
+        way = (1 - sign) // 2
+        return x_copy(
+            sibling - 2 * sign * k, sib_send.at[way, k], sib_recv.at[way, k], sibling
+        )
+
+    def relay(k):
+        for sign in (1, -1):
+
+            @pl.when(reaches(-sign, k))
+            def _():
+                if k > 0:
+                    landed(sign, k).wait_recv()
+                if k + 1 < chips:
+
+                    @pl.when(reaches(sign, 1))
+                    def _():
+                        hop(sign, k).start()
+
+                if k > 0:
+                    hand_over(sign, k).start()
+
+    relay(0)
+    hand_over(1, 0).start()
     send_own(0)
     send_own(1)
-    sib_out[0].start()
+    relay(1)
     pass_on(0)
     for i in range(2, n_var):
         send_own(i)
-    pass_on(1)
-    for k in range(chips - 1):
-        x_copy(far_from[k], x_send.at[k], x_recv.at[k], far[k]).wait_recv()
-        copy = x_copy(far_from[k], sib_send.at[k + 1], sib_recv.at[k + 1], sibling)
-        copy.start()
-        sib_out.append(copy)
-    sib_from = [sibling] + [(sibling + n_mut - 2 * k) % n_mut for k in range(1, chips)]
-    for k in range(chips):
-        x_copy(sib_from[k], sib_send.at[k], sib_recv.at[k], sibling).wait_recv()
+    for k in range(2, chips):
+        relay(k)
+        if k < 4:
+            pass_on(k - 1)
+    handed(1, 0).wait_recv()
+    for k in range(1, chips):
+        for sign in (1, -1):
+
+            @pl.when(reaches(-sign, k))
+            def _():
+                handed(sign, k).wait_recv()
+
     for copy in local:
         copy.wait()
 
@@ -171,7 +224,7 @@
             number = (entry // img_dev * n_test + t) * img_dev + entry % img_dev
             labels[i, pl.ds(j, 1), :] = jnp.full((1, 128), label_ref[number], jnp.int32)
         for step in range(steps):
-            strength = strength_ref[i, step]
+            strength = strength_ref[step, i]
             for part in range(n_test):
                 span = pl.ds(part * block, block)
                 w1_step[span, :] = (
@@ -196,17 +249,20 @@
                 ).astype(BF16)
         if square:
 
-            @pl.when(i + 2 < n_var)
+            @pl.when(i + 3 < n_var)
             def _():
-                pass_on(i + 2)
+                pass_on(i + 3)
 
         return carry
 
     lax.fori_loop(0, n_var, variant, 0)
 
     count = n_var * steps * padded
-    logits = jnp.dot(
-        pooled[...].reshape(count, width), readout[...], preferred_element_type=F32
+    logits = lax.dot_general(
+        pooled[...].reshape(count, width),
+        readout[...],
+        (((1,), (1,)), ((), ())),
+        preferred_element_type=F32,
     )
     classes = logits.shape[1]
     top = jnp.max(logits, axis=1, keepdims=True)
@@ -225,8 +281,20 @@
     for i in range(n_var):
         kill_ref[i] = spread[i * steps : (i + 1) * steps, :surv]
 
-    for copy in x_out + sib_out:
-        copy.wait_send()
+    hand_over(1, 0).wait_send()
+    for k in range(chips):
+        for sign in (1, -1):
+
+            @pl.when(reaches(-sign, k))
+            def _():
+                if k > 0:
+                    hand_over(sign, k).wait_send()
+                if k + 1 < chips:
+
+                    @pl.when(reaches(sign, 1))
+                    def _():
+                        hop(sign, k).wait_send()
+
 
     def drain(i, carry):
         for which in range(2):
@@ -255,7 +323,7 @@
         chips = n_mut // 2
         smem = pl.BlockSpec(memory_space=pltpu.SMEM)
         vmem = pl.BlockSpec(memory_space=pltpu.VMEM)
-        anywhere = pl.BlockSpec(memory_space=pl.ANY)
+        anywhere = pl.BlockSpec(memory_space=pltpu.HBM)
         macs = n_var * steps * surv * slot * width * narrow * 2
         return pl.pallas_call(
             functools.partial(kernel, n_mut, n_test),
@@ -268,26 +336,26 @@
                 pltpu.VMEM((n_var, n_test, narrow, block), BF16),
                 pltpu.VMEM(w1.shape, BF16),
                 pltpu.VMEM(w2.shape, BF16),
-                pltpu.VMEM(readout.shape, BF16),
+                pltpu.VMEM(readout.shape[::-1], BF16),
                 pltpu.VMEM((surv * slot, width), BF16),
                 pltpu.VMEM((width, narrow), BF16),
                 pltpu.VMEM((n_var * steps, padded, width), BF16),
                 pltpu.VMEM((n_var, padded, 128), jnp.int32),
                 dma((5,)),
-                dma((chips,)),
-                dma((chips,)),
-                dma((chips,)),
-                dma((chips,)),
+                dma((2, chips)),
+                dma((2, chips)),
+                dma((2, chips)),
+                dma((2, chips)),
                 dma((2, n_var, places)),
                 dma((2, n_var, places)),
             ],
             compiler_params=pltpu.CompilerParams(
-                collective_id=0, has_side_effects=True, vmem_limit_bytes=48 * 2**20
+                collective_id=0, has_side_effects=True, vmem_limit_bytes=60 * 2**20
             ),
             cost_estimate=pl.CostEstimate(
                 flops=2 * macs, bytes_accessed=8 * 2**20, transcendentals=0
             ),
-        )(left, strength, label, x, d1, d2, w1, w2, readout)
+        )(left, strength.T, label, x.transpose(1, 0, 2), d1, d2, w1, w2, readout.T)
 
     return jax.shard_map(
         on_device,

time: 53.9 us -> 45.5 us (0.84)
  local copies, waits for them, and re-layouts: 7.4 us -> 1.28 us
  Pallas kernels: 46.1 us -> 44 us
    unnamed x16 -> x1, local copies, waits for them, and re-layouts: 7.4 us -> 1.28 us
    pallas_call x1, Pallas kernels: 46.1 us -> 44 us  [on_device(): pl.pallas_call(functools.partial(kernel, n_mut, n_test), out_shape=jax.Sh...]
where the time goes in v2:
time: 45.5 us; the launch traced here: 45.3 us
  Pallas kernels  44 us (97%)
  local copies, waits for them, and re-layouts  1.28 us (3%)
    pallas_call x1, Pallas kernels, on_device(): pl.pallas_call(functools.partial(kernel, n_mut, n_test), out_shape=jax.Sh...  44 us
    unnamed x1, local copies, waits for them, and re-layouts  1.28 us

profile of v2, /device:TPU:0, one launch (start us, length us, event | category | flops | bytes accessed | tf_op | source)
XLA Modules:
  0.0 45.3 jit_solution(4484371079810247633)
XLA Ops:
  0.0 44.0 %shard_map.91 = f32[4,2,14]{2,1,0:T(2,128)} custom-call(s32[4,14]{1,0:T(4,128)} %left_ref.1, f32[2,4]{1,0:T(2,128)} %bitcast.5, s32[128]{0:T(128)} %label_ref.1, bf16[28,4,1024]{2,1,0:T(4,128)(2,1)} %bitcast.4, bf16[4,256,256]{2,1,0:T(8,128)(2,1)} %d1_ref.1, bf16[4,256,256]{2,1,0:T(8,128)(2,1)} %d2_ref.1, bf16[1024,256]{1,0:T(8,128)(2,1)} %w1_ref.1, ...), custom_call_target="tpu_custom_call" | custom-call | flops 3758096384 | bytes 8388608 | tf_op jit(solution)/shard_map/pallas_call | solution.py:328
  44.1 1.3 %copy.11 = f32[4,2,14]{2,1,0:T(2,128)} copy(f32[4,2,14]{2,1,0:T(2,128)} %shard_map.91) | data formatting | bytes 896

commit v3 on v2

--- a/solution.py
+++ b/solution.py
@@ -19,6 +19,7 @@
     n_mut,
     n_test,
     left_ref,
+    left_rows,
     strength_ref,
     label_ref,
     x_ref,
@@ -29,6 +30,7 @@
     readout_ref,
     kill_ref,
     images,
+    images2,
     d1_all,
     d2_all,
     w1,
@@ -45,6 +47,19 @@
     sib_recv,
     d_send,
     d_recv,
+    cross_send,
+    cross_recv,
+    half_send,
+    half_recv,
+    sib2_send,
+    sib2_recv,
+    extra_send,
+    extra_recv,
+    table_out,
+    table_in,
+    table,
+    scores_out,
+    scores_in,
 ):
     pix, img_dev, width = x_ref.shape
     slot = images.shape[1]
@@ -57,7 +72,11 @@
     chips = n_mut // 2
     sibling = m + 1 - 2 * (m % 2)
     chip = m // 2
-    square = n_test == 4
+    square = n_test == 4 and n_var % 2 == 0
+    mine = n_var // 2 if square else n_var
+    shards = 2 if square else 1
+    first = (t % 2) * mine if square else 0
+    half = img_dev // 2
     if square:
         across, along = t + 1 - 2 * (t % 2), (t + 2) % 4
         near = [across, along]
@@ -73,8 +92,8 @@
         pltpu.make_async_copy(w1_ref, w1, local_sem.at[0]),
         pltpu.make_async_copy(w2_ref, w2, local_sem.at[1]),
         pltpu.make_async_copy(readout_ref, readout, local_sem.at[2]),
-        pltpu.make_async_copy(d1_ref, d1_all.at[:, t], local_sem.at[3]),
-        pltpu.make_async_copy(d2_ref, d2_all.at[:, t], local_sem.at[4]),
+        pltpu.make_async_copy(d1_ref.at[pl.ds(first, mine)], d1_all.at[:, t], local_sem.at[3]),
+        pltpu.make_async_copy(d2_ref.at[pl.ds(first, mine)], d2_all.at[:, t], local_sem.at[4]),
     ]
 
     barrier = pltpu.get_barrier_semaphore()
@@ -95,20 +114,35 @@
         images[m * img_dev + j] = jnp.concatenate(
             [x_ref[:, j, :], jnp.zeros((slot - pix, width), BF16)], axis=0
         )
+    if square:
+        table_out[...] = jnp.zeros_like(table_out)
+        table_out[0:n_var, 0:surv] = left_rows[...]
     below = (chip + chips - 1) // chips
     above = (2 * chips - 2 - chip) // chips
     pl.semaphore_wait(barrier, 1 + len(near) + below + above)
 
-    def x_copy(source, send, recv, target):
-        view = images.at[pl.ds(source * img_dev, img_dev)]
+    def x_copy(source, send, recv, target, shard=0, low=0, count=img_dev):
+        held = images2 if shard else images
+        view = held.at[pl.ds(source * img_dev + low, count)]
         return pltpu.make_async_remote_copy(
             view, view, send, recv, device_id=(target, t), device_id_type=MESH
         )
 
+    def cross_copy(source, send, recv, low, count):
+        return pltpu.make_async_remote_copy(
+            images.at[pl.ds(source * img_dev + low, count)],
+            images2.at[pl.ds(source * img_dev + low, count)],
+            send,
+            recv,
+            device_id=(m, across),
+            device_id_type=MESH,
+        )
+
     def own_copy(which, i, place):
         ref, full = ((d1_ref, d1_all), (d2_ref, d2_all))[which]
+        start = mine - first if square and place == 0 else first
         return pltpu.make_async_remote_copy(
-            ref.at[i],
+            ref.at[start + i],
             full.at[i, t],
             d_send.at[which, i, place],
             d_recv.at[which, i, place],
@@ -144,11 +178,9 @@
                 own_copy(which, i, place).start()
 
     def pass_on(i):
-        if square:
-            arrived(0, i, 0)
-            held_copy(0, i, 0, along).start()
-            arrived(1, i, 1)
-            held_copy(1, i, 1, across).start()
+        for which in range(2):
+            arrived(which, i, 0)
+            held_copy(which, i, 0, along).start()
 
     def hop(sign, k):
         way = (1 - sign) // 2
@@ -172,6 +204,52 @@
         way = (1 - sign) // 2
         return x_copy(
             sibling - 2 * sign * k, sib_send.at[way, k], sib_recv.at[way, k], sibling
+        )
+
+    def cross_back(sign, k):
+        way = (1 - sign) // 2
+        return cross_copy(
+            m - 2 * sign * k,
+            cross_send.at[way, k],
+            cross_recv.at[way, k],
+            half,
+            img_dev - half,
+        )
+
+    def half_hop(sign, k):
+        way = (1 - sign) // 2
+        return x_copy(
+            m - 2 * sign * k,
+            half_send.at[way, k],
+            half_recv.at[way, k + 1],
+            m + 2 * sign,
+            1,
+            0,
+            half,
+        )
+
+    def half_landed(sign, k):
+        way = (1 - sign) // 2
+        return x_copy(
+            m - 2 * sign * k,
+            half_send.at[way, k],
+            half_recv.at[way, k],
+            m + 2 * sign,
+            1,
+            0,
+            half,
+        )
+
+    def second(origin_core, sign, k, piece):
+        way = (1 - sign) // 2
+        return x_copy(
+            origin_core - 2 * sign * k,
+            sib2_send.at[piece, way, k],
+            sib2_recv.at[piece, way, k],
+            sibling,
+            1,
+            piece * half,
+            img_dev - half if piece else half,
         )
 
     def relay(k):
@@ -188,20 +266,85 @@
                         hop(sign, k).start()
 
                 if k > 0:
+                    if square:
+                        cross_back(sign, k).start()
                     hand_over(sign, k).start()
+
+    def relay_half(k):
+        for sign in (1, -1):
+
+            @pl.when(reaches(-sign, k))
+            def _():
+                if k > 0:
+                    half_landed(sign, k).wait_recv()
+                if k + 1 < chips:
+
+                    @pl.when(reaches(sign, 1))
+                    def _():
+                        half_hop(sign, k).start()
+
+                if k > 0:
+                    second(m, sign, k, 0).start()
+
+    def share_cross(k):
+        for sign in (1, -1):
+
+            @pl.when(reaches(-sign, k))
+            def _():
+                cross_back(sign, k).wait_recv()
+                second(m, sign, k, 1).start()
+
+    def own_cross():
+        return cross_copy(m, extra_send.at[0], extra_recv.at[0], 0, img_dev)
+
+    def own_second(core):
+        return x_copy(core, extra_send.at[1], extra_recv.at[1], sibling, 1)
+
+    def send_table():
+        return pltpu.make_async_remote_copy(
+            table_out,
+            table_in,
+            extra_send.at[2],
+            extra_recv.at[2],
+            device_id=(m, across),
+            device_id_type=MESH,
+        )
+
+    def send_scores():
+        return pltpu.make_async_remote_copy(
+            scores_out,
+            scores_in,
+            extra_send.at[3],
+            extra_recv.at[3],
+            device_id=(m, across),
+            device_id_type=MESH,
+        )
 
     relay(0)
     hand_over(1, 0).start()
-    send_own(0)
-    send_own(1)
-    relay(1)
-    pass_on(0)
-    for i in range(2, n_var):
+    for i in range(mine):
         send_own(i)
-    for k in range(2, chips):
-        relay(k)
-        if k < 4:
-            pass_on(k - 1)
+    if square:
+        own_cross().start()
+        send_table().start()
+        for k in range(1, chips):
+            if k - 1 < mine:
+                pass_on(k - 1)
+            if k == chips - 1:
+                own_cross().wait_recv()
+                relay_half(0)
+                own_second(m).start()
+            relay(k)
+        for i in range(max(chips - 1, 0), mine):
+            pass_on(i)
+        send_table().wait_recv()
+        read_table = pltpu.make_async_copy(table_in, table, local_sem.at[5])
+        read_table.start()
+        read_table.wait()
+        relay_half(1)
+    else:
+        for k in range(1, chips):
+            relay(k)
     handed(1, 0).wait_recv()
     for k in range(1, chips):
         for sign in (1, -1):
@@ -210,21 +353,66 @@
             def _():
                 handed(sign, k).wait_recv()
 
+    def rest(early):
+        if early:
+            relay_half(2)
+            share_cross(1)
+            return
+        for k in range(3, chips):
+            relay_half(k)
+        for k in range(2, chips):
+            share_cross(k)
+        own_second(sibling).wait_recv()
+        for k in range(1, chips):
+            for sign in (1, -1):
+
+                @pl.when(reaches(-sign, k))
+                def _():
+                    for piece in range(2):
+                        second(sibling, sign, k, piece).wait_recv()
+
     for copy in local:
         copy.wait()
 
-    def variant(i, carry):
-        for place in range(len(origin)):
+    def variant(q, carry):
+        i = q % mine
+        if square:
+
+            @pl.when(q == 1)
+            def _():
+                rest(True)
+
+            @pl.when(q == mine)
+            def _():
+                rest(False)
+
+        @pl.when(q < mine)
+        def _():
             for which in range(2):
-                if not (square and place == which):
+                for place in range(1 if square else 0, len(origin)):
                     arrived(which, i, place)
-        for j in range(surv):
-            entry = left_ref[i, j]
-            rows[pl.ds(j * slot, slot), :] = images[entry]
-            number = (entry // img_dev * n_test + t) * img_dev + entry % img_dev
-            labels[i, pl.ds(j, 1), :] = jnp.full((1, 128), label_ref[number], jnp.int32)
+
+        def gather(held, entries, test):
+            for j in range(surv):
+                entry = entries[first + i, j]
+                rows[pl.ds(j * slot, slot), :] = held[entry]
+                number = (entry // img_dev * n_test + test) * img_dev + entry % img_dev
+                labels[q, pl.ds(j, 1), :] = jnp.full(
+                    (1, 128), label_ref[number], jnp.int32
+                )
+
+        @pl.when(q < mine)
+        def _():
+            gather(images, left_ref, t)
+
+        if square:
+
+            @pl.when(q >= mine)
+            def _():
+                gather(images2, table, across)
+
         for step in range(steps):
-            strength = strength_ref[step, i]
+            strength = strength_ref[step, first + i]
             for part in range(n_test):
                 span = pl.ds(part * block, block)
                 w1_step[span, :] = (
@@ -244,20 +432,15 @@
                     0.0,
                 )
                 mean = jnp.sum(out.reshape(surv, slot, block), axis=1) * (1.0 / pix)
-                pooled[i * steps + step, :, span] = jnp.concatenate(
+                pooled[q * steps + step, :, span] = jnp.concatenate(
                     [mean, jnp.zeros((padded - surv, block), F32)], axis=0
                 ).astype(BF16)
-        if square:
-
-            @pl.when(i + 3 < n_var)
-            def _():
-                pass_on(i + 3)
-
         return carry
 
-    lax.fori_loop(0, n_var, variant, 0)
-
-    count = n_var * steps * padded
+    groups = mine * shards
+    lax.fori_loop(0, groups, variant, 0)
+
+    count = groups * steps * padded
     logits = lax.dot_general(
         pooled[...].reshape(count, width),
         readout[...],
@@ -268,7 +451,7 @@
     top = jnp.max(logits, axis=1, keepdims=True)
     total = top + jnp.log(jnp.sum(jnp.exp(logits - top), axis=1, keepdims=True))
     wanted = jnp.concatenate(
-        [labels[i // steps][:, 0:1] for i in range(n_var * steps)], axis=0
+        [labels[i // steps][:, 0:1] for i in range(groups * steps)], axis=0
     )
     column = lax.broadcasted_iota(jnp.int32, (count, classes), 1)
     chosen = jnp.sum(jnp.where(column == wanted, logits, 0.0), axis=1, keepdims=True)
@@ -276,10 +459,18 @@
     row = lax.broadcasted_iota(jnp.int32, (count, 128), 0) % padded
     lane = lax.broadcasted_iota(jnp.int32, (count, 128), 1)
     spread = jnp.sum(
-        jnp.where(row == lane, kill, 0.0).reshape(n_var * steps, padded, 128), axis=1
+        jnp.where(row == lane, kill, 0.0).reshape(groups * steps, padded, 128), axis=1
     )
-    for i in range(n_var):
-        kill_ref[i] = spread[i * steps : (i + 1) * steps, :surv]
+    if square:
+        scores_out[...] = spread
+        send_scores().start()
+    for i in range(mine):
+        kill_ref[first + i] = spread[i * steps : (i + 1) * steps, :surv]
+    if square:
+        send_scores().wait_recv()
+        for i in range(mine):
+            low = (mine + i) * steps
+            kill_ref[mine - first + i] = scores_in[low : low + steps, :surv]
 
     hand_over(1, 0).wait_send()
     for k in range(chips):
@@ -300,12 +491,30 @@
         for which in range(2):
             for place in range(len(near)):
                 own_copy(which, i, place).wait_send()
-        if square:
-            held_copy(0, i, 0, along).wait_send()
-            held_copy(1, i, 1, across).wait_send()
+            if square:
+                held_copy(which, i, 0, along).wait_send()
         return carry
 
-    lax.fori_loop(0, n_var, drain, 0)
+    lax.fori_loop(0, mine, drain, 0)
+    if square:
+        own_cross().wait_send()
+        own_second(m).wait_send()
+        send_table().wait_send()
+        send_scores().wait_send()
+        for k in range(chips):
+            for sign in (1, -1):
+
+                @pl.when(reaches(-sign, k))
+                def _():
+                    if k > 0:
+                        cross_back(sign, k).wait_send()
+                        second(m, sign, k, 0).wait_send()
+                        second(m, sign, k, 1).wait_send()
+                    if k + 1 < chips:
+
+                        @pl.when(reaches(sign, 1))
+                        def _():
+                            half_hop(sign, k).wait_send()
 
 
 def solution(mesh):
@@ -320,6 +529,9 @@
         padded = round_up(surv, 16)
         dma = pltpu.SemaphoreType.DMA
         places = max(3, n_test - 1)
+        square = n_test == 4 and n_var % 2 == 0
+        mine = n_var // 2 if square else n_var
+        groups = n_var
         chips = n_mut // 2
         smem = pl.BlockSpec(memory_space=pltpu.SMEM)
         vmem = pl.BlockSpec(memory_space=pltpu.VMEM)
@@ -328,26 +540,40 @@
         return pl.pallas_call(
             functools.partial(kernel, n_mut, n_test),
             out_shape=jax.ShapeDtypeStruct((n_var, steps, surv), F32),
-            in_specs=[smem, smem, smem, vmem] + [anywhere] * 5,
+            in_specs=[smem, vmem, smem, smem, vmem] + [anywhere] * 5,
             out_specs=vmem,
             scratch_shapes=[
                 pltpu.VMEM((n_mut * img_dev, slot, width), BF16),
-                pltpu.VMEM((n_var, n_test, block, narrow), BF16),
-                pltpu.VMEM((n_var, n_test, narrow, block), BF16),
+                pltpu.VMEM((n_mut * img_dev, slot, width), BF16),
+                pltpu.VMEM((mine, n_test, block, narrow), BF16),
+                pltpu.VMEM((mine, n_test, narrow, block), BF16),
                 pltpu.VMEM(w1.shape, BF16),
                 pltpu.VMEM(w2.shape, BF16),
                 pltpu.VMEM(readout.shape[::-1], BF16),
                 pltpu.VMEM((surv * slot, width), BF16),
                 pltpu.VMEM((width, narrow), BF16),
-                pltpu.VMEM((n_var * steps, padded, width), BF16),
-                pltpu.VMEM((n_var, padded, 128), jnp.int32),
-                dma((5,)),
+                pltpu.VMEM((groups * steps, padded, width), BF16),
+                pltpu.VMEM((groups, padded, 128), jnp.int32),
+                dma((6,)),
                 dma((2, chips)),
                 dma((2, chips)),
                 dma((2, chips)),
                 dma((2, chips)),
                 dma((2, n_var, places)),
                 dma((2, n_var, places)),
+                dma((2, chips)),
+                dma((2, chips)),
+                dma((2, chips)),
+                dma((2, chips)),
+                dma((2, 2, chips)),
+                dma((2, 2, chips)),
+                dma((4,)),
+                dma((4,)),
+                pltpu.VMEM((round_up(n_var, 8), 128), jnp.int32),
+                pltpu.VMEM((round_up(n_var, 8), 128), jnp.int32),
+                pltpu.SMEM((round_up(n_var, 8), 128), jnp.int32),
+                pltpu.VMEM((groups * steps, 128), F32),
+                pltpu.VMEM((groups * steps, 128), F32),
             ],
             compiler_params=pltpu.CompilerParams(
                 collective_id=0, has_side_effects=True, vmem_limit_bytes=60 * 2**20
@@ -355,7 +581,7 @@
             cost_estimate=pl.CostEstimate(
                 flops=2 * macs, bytes_accessed=8 * 2**20, transcendentals=0
             ),
-        )(left, strength.T, label, x.transpose(1, 0, 2), d1, d2, w1, w2, readout.T)
+        )(left, left, strength.T, label, x.transpose(1, 0, 2), d1, d2, w1, w2, readout.T)
 
     return jax.shard_map(
         on_device,

time: 45.5 us -> 48.7 us (1.070)
  Pallas kernels: 44 us -> 46.8 us
    pallas_call x1, Pallas kernels: 44 us -> 46.8 us  [on_device(): pl.pallas_call(functools.partial(kernel, n_mut, n_test), out_shape=jax.Sh...]
where the time goes in v3:
time: 48.7 us; the launch traced here: 48.1 us
  Pallas kernels  46.8 us (96%)
  local copies, waits for them, and re-layouts  1.28 us (3%)
    pallas_call x1, Pallas kernels, on_device(): pl.pallas_call(functools.partial(kernel, n_mut, n_test), out_shape=jax.Sh...  46.8 us
    unnamed x1, local copies, waits for them, and re-layouts  1.28 us

profile of v3, /device:TPU:0, one launch (start us, length us, event | category | flops | bytes accessed | tf_op | source)
XLA Modules:
  0.0 48.1 jit_solution(2849430400161522177)
XLA Ops:
  0.0 46.8 %shard_map.91 = f32[4,2,14]{2,1,0:T(2,128)} custom-call(s32[4,14]{1,0:T(4,128)} %left_rows.1, s32[4,14]{1,0:T(4,128)} %left_rows.1, f32[2,4]{1,0:T(2,128)} %bitcast.5, s32[128]{0:T(128)} %label_ref.1, bf16[28,4,1024]{2,1,0:T(4,128)(2,1)} %bitcast.4, bf16[4,256,256]{2,1,0:T(8,128)(2,1)} %d1_ref.1, bf16[4,256,256]{2,1,0:T(8,128)(2,1)} %d2_ref.1, ...), custom_call_target="tpu_custom_call" | custom-call | flops 3758096384 | bytes 8388608 | tf_op jit(solution)/shard_map/pallas_call | solution.py:540
  46.8 1.3 %copy.11 = f32[4,2,14]{2,1,0:T(2,128)} copy(f32[4,2,14]{2,1,0:T(2,128)} %shard_map.91) | data formatting | bytes 896

commit v4 on v3

--- a/solution.py
+++ b/solution.py
@@ -38,6 +38,7 @@
     readout,
     rows,
     w1_step,
+    w2_step,
     pooled,
     labels,
     local_sem,
@@ -345,14 +346,6 @@
     else:
         for k in range(1, chips):
             relay(k)
-    handed(1, 0).wait_recv()
-    for k in range(1, chips):
-        for sign in (1, -1):
-
-            @pl.when(reaches(-sign, k))
-            def _():
-                handed(sign, k).wait_recv()
-
     def rest(early):
         if early:
             relay_half(2)
@@ -362,6 +355,7 @@
             relay_half(k)
         for k in range(2, chips):
             share_cross(k)
+        keep_own()
         own_second(sibling).wait_recv()
         for k in range(1, chips):
             for sign in (1, -1):
@@ -371,8 +365,48 @@
                     for piece in range(2):
                         second(sibling, sign, k, piece).wait_recv()
 
-    for copy in local:
-        copy.wait()
+    def finish(base, number):
+        count = number * padded
+        logits = lax.dot_general(
+            pooled[base : base + number].reshape(count, width),
+            readout[...],
+            (((1,), (1,)), ((), ())),
+            preferred_element_type=F32,
+        )
+        classes = logits.shape[1]
+        top = jnp.max(logits, axis=1, keepdims=True)
+        total = top + jnp.log(jnp.sum(jnp.exp(logits - top), axis=1, keepdims=True))
+        wanted = jnp.concatenate(
+            [labels[i // steps][:, 0:1] for i in range(base, base + number)], axis=0
+        )
+        column = lax.broadcasted_iota(jnp.int32, (count, classes), 1)
+        chosen = jnp.sum(jnp.where(column == wanted, logits, 0.0), axis=1, keepdims=True)
+        kill = total - chosen
+        row = lax.broadcasted_iota(jnp.int32, (count, 128), 0) % padded
+        lane = lax.broadcasted_iota(jnp.int32, (count, 128), 1)
+        return jnp.sum(
+            jnp.where(row == lane, kill, 0.0).reshape(number, padded, 128), axis=1
+        )
+
+    def keep_own():
+        spread = finish(0, mine * steps)
+        for i in range(mine):
+            kill_ref[first + i] = spread[i * steps : (i + 1) * steps, :surv]
+
+    def build(i):
+        for which in range(2):
+            for place in range(1 if square else 0, len(origin)):
+                arrived(which, i, place)
+        for part in range(n_test):
+            span = pl.ds(part * block, block)
+            base1, delta1 = w1[span, :].astype(F32), d1_all[i, part].astype(F32)
+            base2, delta2 = w2[:, span].astype(F32), d2_all[i, part].astype(F32)
+            for step in range(steps):
+                strength = strength_ref[step, first + i]
+                w1_step[i, span, pl.ds(step * narrow, narrow)] = (
+                    base1 + strength * delta1
+                ).astype(BF16)
+                w2_step[i, step, :, span] = (base2 + strength * delta2).astype(BF16)
 
     def variant(q, carry):
         i = q % mine
@@ -386,11 +420,9 @@
             def _():
                 rest(False)
 
-        @pl.when(q < mine)
+        @pl.when((q > 0) & (q < mine))
         def _():
-            for which in range(2):
-                for place in range(1 if square else 0, len(origin)):
-                    arrived(which, i, place)
+            build(i)
 
         def gather(held, entries, test):
             for j in range(surv):
@@ -411,66 +443,50 @@
             def _():
                 gather(images2, table, across)
 
-        for step in range(steps):
-            strength = strength_ref[step, first + i]
-            for part in range(n_test):
-                span = pl.ds(part * block, block)
-                w1_step[span, :] = (
-                    w1[span, :].astype(F32) + strength * d1_all[i, part].astype(F32)
-                ).astype(BF16)
-            hidden = jnp.maximum(
-                jnp.dot(rows[...], w1_step[...], preferred_element_type=F32), 0.0
-            ).astype(BF16)
-            for part in range(n_test):
-                span = pl.ds(part * block, block)
-                w2_step = (
-                    w2[:, span].astype(F32) + strength * d2_all[i, part].astype(F32)
-                ).astype(BF16)
+        hidden = jnp.maximum(
+            jnp.dot(rows[...], w1_step[i], preferred_element_type=F32), 0.0
+        ).astype(BF16)
+        for low in range(0, width, narrow):
+            span = pl.ds(low, narrow)
+            residual = rows[:, span].astype(F32)
+            for step in range(steps):
                 out = jnp.maximum(
-                    jnp.dot(hidden, w2_step, preferred_element_type=F32)
-                    + rows[:, span].astype(F32),
+                    jnp.dot(
+                        hidden[:, step * narrow : (step + 1) * narrow],
+                        w2_step[i, step, :, span],
+                        preferred_element_type=F32,
+                    )
+                    + residual,
                     0.0,
                 )
-                mean = jnp.sum(out.reshape(surv, slot, block), axis=1) * (1.0 / pix)
+                mean = jnp.sum(out.reshape(surv, slot, narrow), axis=1) * (1.0 / pix)
                 pooled[q * steps + step, :, span] = jnp.concatenate(
-                    [mean, jnp.zeros((padded - surv, block), F32)], axis=0
+                    [mean, jnp.zeros((padded - surv, narrow), F32)], axis=0
                 ).astype(BF16)
         return carry
 
+    for copy in local:
+        copy.wait()
+    build(0)
+    handed(1, 0).wait_recv()
+    for k in range(1, chips):
+        for sign in (1, -1):
+
+            @pl.when(reaches(-sign, k))
+            def _():
+                handed(sign, k).wait_recv()
+
     groups = mine * shards
     lax.fori_loop(0, groups, variant, 0)
 
-    count = groups * steps * padded
-    logits = lax.dot_general(
-        pooled[...].reshape(count, width),
-        readout[...],
-        (((1,), (1,)), ((), ())),
-        preferred_element_type=F32,
-    )
-    classes = logits.shape[1]
-    top = jnp.max(logits, axis=1, keepdims=True)
-    total = top + jnp.log(jnp.sum(jnp.exp(logits - top), axis=1, keepdims=True))
-    wanted = jnp.concatenate(
-        [labels[i // steps][:, 0:1] for i in range(groups * steps)], axis=0
-    )
-    column = lax.broadcasted_iota(jnp.int32, (count, classes), 1)
-    chosen = jnp.sum(jnp.where(column == wanted, logits, 0.0), axis=1, keepdims=True)
-    kill = total - chosen
-    row = lax.broadcasted_iota(jnp.int32, (count, 128), 0) % padded
-    lane = lax.broadcasted_iota(jnp.int32, (count, 128), 1)
-    spread = jnp.sum(
-        jnp.where(row == lane, kill, 0.0).reshape(groups * steps, padded, 128), axis=1
-    )
     if square:
-        scores_out[...] = spread
+        scores_out[...] = finish(mine * steps, mine * steps)
         send_scores().start()
-    for i in range(mine):
-        kill_ref[first + i] = spread[i * steps : (i + 1) * steps, :surv]
-    if square:
         send_scores().wait_recv()
         for i in range(mine):
-            low = (mine + i) * steps
-            kill_ref[mine - first + i] = scores_in[low : low + steps, :surv]
+            kill_ref[mine - first + i] = scores_in[i * steps : (i + 1) * steps, :surv]
+    else:
+        keep_own()
 
     hand_over(1, 0).wait_send()
     for k in range(chips):
@@ -551,7 +567,8 @@
                 pltpu.VMEM(w2.shape, BF16),
                 pltpu.VMEM(readout.shape[::-1], BF16),
                 pltpu.VMEM((surv * slot, width), BF16),
-                pltpu.VMEM((width, narrow), BF16),
+                pltpu.VMEM((mine, width, steps * narrow), BF16),
+                pltpu.VMEM((mine, steps, narrow, width), BF16),
                 pltpu.VMEM((groups * steps, padded, width), BF16),
                 pltpu.VMEM((groups, padded, 128), jnp.int32),
                 dma((6,)),
@@ -572,8 +589,8 @@
                 pltpu.VMEM((round_up(n_var, 8), 128), jnp.int32),
                 pltpu.VMEM((round_up(n_var, 8), 128), jnp.int32),
                 pltpu.SMEM((round_up(n_var, 8), 128), jnp.int32),
-                pltpu.VMEM((groups * steps, 128), F32),
-                pltpu.VMEM((groups * steps, 128), F32),
+                pltpu.VMEM((mine * steps, 128), F32),
+                pltpu.VMEM((mine * steps, 128), F32),
             ],
             compiler_params=pltpu.CompilerParams(
                 collective_id=0, has_side_effects=True, vmem_limit_bytes=60 * 2**20

time: 48.7 us -> 48.4 us (level)
  no operation moved by 1% of the time
where the time goes in v4:
time: 48.4 us; the launch traced here: 48.2 us
  Pallas kernels  47 us (97%)
  local copies, waits for them, and re-layouts  1.28 us (3%)
    pallas_call x1, Pallas kernels, on_device(): pl.pallas_call(functools.partial(kernel, n_mut, n_test), out_shape=jax.Sh...  47 us
    unnamed x1, local copies, waits for them, and re-layouts  1.28 us

profile of v4, /device:TPU:0, one launch (start us, length us, event | category | flops | bytes accessed | tf_op | source)
XLA Modules:
  0.0 48.2 jit_solution(15374859810687476239)
XLA Ops:
  0.0 47.0 %shard_map.91 = f32[4,2,14]{2,1,0:T(2,128)} custom-call(s32[4,14]{1,0:T(4,128)} %left_rows.1, s32[4,14]{1,0:T(4,128)} %left_rows.1, f32[2,4]{1,0:T(2,128)} %bitcast.5, s32[128]{0:T(128)} %label_ref.1, bf16[28,4,1024]{2,1,0:T(4,128)(2,1)} %bitcast.4, bf16[4,256,256]{2,1,0:T(8,128)(2,1)} %d1_ref.1, bf16[4,256,256]{2,1,0:T(8,128)(2,1)} %d2_ref.1, ...), custom_call_target="tpu_custom_call" | custom-call | flops 3758096384 | bytes 8388608 | tf_op jit(solution)/shard_map/pallas_call | solution.py:556
  47.0 1.3 %copy.11 = f32[4,2,14]{2,1,0:T(2,128)} copy(f32[4,2,14]{2,1,0:T(2,128)} %shard_map.91) | data formatting | bytes 896

commit v5 on v4

--- a/solution.py
+++ b/solution.py
@@ -73,7 +73,7 @@
     chips = n_mut // 2
     sibling = m + 1 - 2 * (m % 2)
     chip = m // 2
-    square = n_test == 4 and n_var % 2 == 0
+    square = n_test == 4 and n_var == 4 and chips == 4
     mine = n_var // 2 if square else n_var
     shards = 2 if square else 1
     first = (t % 2) * mine if square else 0
@@ -323,37 +323,42 @@
 
     relay(0)
     hand_over(1, 0).start()
-    for i in range(mine):
-        send_own(i)
+    send_own(0)
     if square:
         own_cross().start()
         send_table().start()
-        for k in range(1, chips):
-            if k - 1 < mine:
-                pass_on(k - 1)
-            if k == chips - 1:
-                own_cross().wait_recv()
-                relay_half(0)
-                own_second(m).start()
+        relay(1)
+        for i in range(1, mine):
+            send_own(i)
+        own_cross().wait_recv()
+        relay_half(0)
+        own_second(m).start()
+        pass_on(0)
+        relay(2)
+        relay_half(1)
+        pass_on(1)
+        for k in range(3, chips):
             relay(k)
-        for i in range(max(chips - 1, 0), mine):
+        for i in range(2, mine):
             pass_on(i)
         send_table().wait_recv()
         read_table = pltpu.make_async_copy(table_in, table, local_sem.at[5])
         read_table.start()
         read_table.wait()
-        relay_half(1)
+        relay_half(2)
     else:
+        for i in range(1, mine):
+            send_own(i)
         for k in range(1, chips):
             relay(k)
     def rest(early):
         if early:
-            relay_half(2)
+            for k in range(3, chips):
+                relay_half(k)
             share_cross(1)
+            share_cross(2)
             return
         for k in range(3, chips):
-            relay_half(k)
-        for k in range(2, chips):
             share_cross(k)
         keep_own()
         own_second(sibling).wait_recv()
@@ -545,10 +550,10 @@
         padded = round_up(surv, 16)
         dma = pltpu.SemaphoreType.DMA
         places = max(3, n_test - 1)
-        square = n_test == 4 and n_var % 2 == 0
+        chips = n_mut // 2
+        square = n_test == 4 and n_var == 4 and chips == 4
         mine = n_var // 2 if square else n_var
         groups = n_var
-        chips = n_mut // 2
         smem = pl.BlockSpec(memory_space=pltpu.SMEM)
         vmem = pl.BlockSpec(memory_space=pltpu.VMEM)
         anywhere = pl.BlockSpec(memory_space=pltpu.HBM)

time: 48.4 us -> 47.6 us (0.983)
  Pallas kernels: 47 us -> 46.1 us
    pallas_call x1, Pallas kernels: 47 us -> 46.1 us  [on_device(): pl.pallas_call(functools.partial(kernel, n_mut, n_test), out_shape=jax.Sh...]
where the time goes in v5:
time: 47.6 us; the launch traced here: 47.4 us
  Pallas kernels  46.1 us (97%)
  local copies, waits for them, and re-layouts  1.28 us (3%)
    pallas_call x1, Pallas kernels, on_device(): pl.pallas_call(functools.partial(kernel, n_mut, n_test), out_shape=jax.Sh...  46.1 us
    unnamed x1, local copies, waits for them, and re-layouts  1.28 us

profile of v5, /device:TPU:0, one launch (start us, length us, event | category | flops | bytes accessed | tf_op | source)
XLA Modules:
  0.0 47.4 jit_solution(14710719427282733936)
XLA Ops:
  0.0 46.1 %shard_map.91 = f32[4,2,14]{2,1,0:T(2,128)} custom-call(s32[4,14]{1,0:T(4,128)} %left_rows.1, s32[4,14]{1,0:T(4,128)} %left_rows.1, f32[2,4]{1,0:T(2,128)} %bitcast.5, s32[128]{0:T(128)} %label_ref.1, bf16[28,4,1024]{2,1,0:T(4,128)(2,1)} %bitcast.4, bf16[4,256,256]{2,1,0:T(8,128)(2,1)} %d1_ref.1, bf16[4,256,256]{2,1,0:T(8,128)(2,1)} %d2_ref.1, ...), custom_call_target="tpu_custom_call" | custom-call | flops 3758096384 | bytes 8388608 | tf_op jit(solution)/shard_map/pallas_call | solution.py:561
  46.2 1.3 %copy.11 = f32[4,2,14]{2,1,0:T(2,128)} copy(f32[4,2,14]{2,1,0:T(2,128)} %shard_map.91) | data formatting | bytes 896
